TPU v7x, 32 devices: a whole 2x2x4 slice. The times are simulated.
32 devices in a mesh: gx: 8 (over z, x), yz: 4 (over y, core).
Axes of the slice: x: 2, y: 2, z: 4, core: 2. Of those that a mesh axis runs over, the one named last changes fastest.
Arguments:
- tensor_slabs: bfloat16 [512, 16, 1024], P('gx', 'yz'), may hold values from -6 to 6
- slab_counts: int32 [4], replicated, may hold values from 1 to 4, 8 in all
- column_scale: float32 [8, 1024], replicated, may hold values from -6 to 6
- samples: int32 [8, 256], replicated, may hold values from 0 to 1023
Outputs:
- basis_factor: float32 [512, 256], P('gx')
- core_tensor: bfloat16 [256, 16, 1024], P(None, 'yz', 'gx')
Inputs may be any that keep to these rules, and one draw needn't show every extreme that they name: `slab_counts`: the counts sum to 8; the largest is exactly 4. Slots at or beyond an index's count hold no slab and are not read.
All inputs are finite; a program needn't handle non-finite values.
Results may differ from a plain program's by a relative error of at most 0.0057.
Values may be sent and summed in bfloat16 or wider, within the bound.
A program may use at most 64 MiB of HBM per device.

v0:
```python
import math

import jax
import jax.numpy as jnp
from jax import lax
from jax.sharding import PartitionSpec as P


def hadamard_columns(picked, length):
    index_rows = jnp.arange(length, dtype=jnp.int32)[:, None]
    picked_row = picked[None, :]
    parity = jnp.zeros((length, picked.shape[0]), jnp.int32)
    for bit_place in range(length.bit_length() - 1):
        parity = parity + jnp.bitwise_and(
            jnp.right_shift(index_rows, bit_place), 1
        ) * jnp.bitwise_and(jnp.right_shift(picked_row, bit_place), 1)
    return (1 - 2 * (parity % 2)).astype(jnp.bfloat16)


def local(tensor_slabs, slab_counts, column_scale, samples):
    row_count, slot_count, column_width = tensor_slabs.shape
    sketch_width = samples.shape[1]
    total_slabs = column_scale.shape[0]
    own_index = lax.axis_index("yz")
    group_numbers = jnp.arange(slab_counts.shape[0], dtype=jnp.int32)
    offset = jnp.sum(jnp.where(group_numbers < own_index, slab_counts, 0))
    own_count = slab_counts[own_index]
    pad_scale = jnp.concatenate(
        [column_scale, jnp.zeros((slot_count, column_width), column_scale.dtype)], 0
    )
    pad_samples = jnp.concatenate([samples, jnp.zeros((slot_count, sketch_width), jnp.int32)], 0)
    own_scale = lax.dynamic_slice_in_dim(pad_scale, offset, slot_count, 0)
    own_samples = lax.dynamic_slice_in_dim(pad_samples, offset, slot_count, 0)

    def add_slab(position, total):
        alive = (position < own_count).astype(jnp.float32)
        piece = lax.dynamic_index_in_dim(tensor_slabs, position, 1, keepdims=False)
        slab_scale = lax.dynamic_index_in_dim(own_scale, position, 0, keepdims=False)
        scaled = (piece.astype(jnp.float32) * slab_scale[None, :]).astype(jnp.bfloat16)
        hadamard_part = hadamard_columns(
            lax.dynamic_index_in_dim(own_samples, position, 0, keepdims=False), column_width
        )
        return total + alive * jnp.dot(scaled, hadamard_part, preferred_element_type=jnp.float32)

    partial_sketch = lax.fori_loop(
        0, slot_count, add_slab, jnp.zeros((row_count, sketch_width), jnp.float32)
    )
    normalizer = 1.0 / math.sqrt(total_slabs * column_width)
    sketch = lax.psum(partial_sketch, "yz") * normalizer
    gram_matrix = lax.psum(jnp.dot(sketch.T, sketch, precision=lax.Precision.HIGHEST), "gx")
    cholesky_factor = jnp.linalg.cholesky(gram_matrix)
    basis_factor = lax.linalg.triangular_solve(
        cholesky_factor, sketch, left_side=False, lower=True, transpose_a=True
    )
    factor_bf = basis_factor.astype(jnp.bfloat16)
    moved = lax.all_to_all(tensor_slabs, "gx", split_axis=2, concat_axis=0, tiled=True)
    every_row = lax.all_gather(factor_bf, "gx", axis=0, tiled=True)
    flattened = moved.reshape(moved.shape[0], moved.shape[1] * moved.shape[2])
    combined = jnp.dot(every_row.T, flattened, preferred_element_type=jnp.float32).reshape(
        sketch_width, moved.shape[1], moved.shape[2]
    )
    slot_alive = (jnp.arange(slot_count, dtype=jnp.int32) < own_count).astype(jnp.float32)
    core_tensor = (combined * slot_alive[None, :, None]).astype(jnp.bfloat16)
    return (basis_factor, core_tensor)


def solution(mesh):
    placed = (P("gx", "yz", None), P(), P(), P())
    return jax.shard_map(
        local,
        mesh=mesh,
        in_specs=placed,
        out_specs=(P("gx", None), P(None, "yz", "gx")),
        check_vma=False,
    )
```

profile of v0, /device:TPU:0, one launch (start us, length us, event | category | flops | bytes accessed | tf_op | source)
XLA Modules:
  0.0 238.2 jit_solution(485945980264843927)
XLA Ops:
  7.2 0.6 copy-done.4
  7.9 0.6 fusion.45
  11.0 0.8 pad_dynamic-slice_fusion
  11.8 14.3 %while.18 = (s32[]{:T(128)}, f32[64,256]{1,0:T(8,128)S(1)}, s32[]{:T(128)}, bf16[64,4,1024]{2,1,0:T(4,128)(2,1)}, f32[4,1024]{1,0:T(4,128)S(1)}, /*index=5*/s32[4,256]{1,0:T(4,128)S(1)}, s32[]{:T(128)}, s32[]{:T(128)}) while((s32[]{:T(128)}, f32[64,256]{1,0:T(8,128)S(1)}, s32[]{:T(128)}, bf16[64,4,1024]{2,1,0:T(4,128)(2,1)}, ...), condition=%wide.region_2.3_spmd.clone, body=%wide.region_1.2_spmd.clone.sunk | while | flops 42476548 | bytes 904325 | solution.py:45
  11.9 1.3 dynamic-slice_convert_fusion.2
  13.8 1.6 fusion.61
  15.5 1.3 dynamic-slice_convert_fusion.2
  17.3 1.6 fusion.61
  19.0 1.3 dynamic-slice_convert_fusion.2
  20.9 1.6 fusion.61
  22.6 1.3 dynamic-slice_convert_fusion.2
  24.5 1.6 fusion.61
  26.1 0.6 copy-done.2
  26.7 1.9 copy.23
  28.6 1.5 reshape.127
  30.1 7.3 %all-to-all-start = ((bf16[8,2,16384]{2,1,0:T(2,128)(2,1)}), bf16[8,2,16384]{2,1,0:T(2,128)(2,1)S(1)}, u32[]{:S(2)}, u32[]{:S(2)}) async-start(bf16[8,2,16384]{2,1,0:T(2,128)(2,1)} %reshape.127), calls=%async_computation | async-start | bytes 1048576 | tf_op jit(solution)/shard_map/all_to_all | solution.py:56
  37.6 23.0 %all-reduce.6.cloned.1.call-done = f32[64,256]{1,0:T(8,128)} async-done(((f32[64,256]{1,0:T(8,128)}), f32[64,256]{1,0:T(8,128)}) %all-reduce.6.cloned.1.call-update) | async-done | bytes 65552 | tf_op jit(solution)/shard_map/psum | solution.py:49
  60.6 2.0 fusion.46
  63.5 72.0 %all-reduce.8.cloned.1.call-done = f32[256,256]{0,1:T(8,128)} async-done(((f32[256,256]{0,1:T(8,128)}), f32[256,256]{0,1:T(8,128)}) %all-reduce.8.cloned.1.call-update) | async-done | bytes 262160 | tf_op jit(solution)/shard_map/psum | solution.py:50
  135.5 1.1 copy.22
  136.7 11.7 %cholesky.50 = f32[128,128]{1,0:T(8,128)S(1)} custom-call(f32[128,128]{1,0:T(8,128)S(1)} %cholesky.118), custom_call_target="Cholesky" | custom-call | tf_op jit(solution)/shard_map/jit(cholesky)/cholesky | solution.py:51
  148.5 9.8 %custom-call.14 = f32[1,128,128]{1,2,0:T(8,128)S(1)} custom-call(f32[1,128,128]{2,1,0:T(8,128)S(1)} %get-tuple-element.243), custom_call_target="InvertDiagBlocksLowerTriangular" | custom-call | tf_op jit(solution)/shard_map/jit(cholesky)/cholesky | solution.py:51
  158.8 11.7 %cholesky.105 = f32[128,128]{1,0:T(8,128)S(1)} custom-call(f32[128,128]{1,0:T(8,128)S(1)} %convolution_subtract_fusion), custom_call_target="Cholesky" | custom-call | tf_op jit(solution)/shard_map/jit(cholesky)/cholesky | solution.py:51
  170.6 0.6 compare_reduce_fusion
  172.6 4.2 %while.17 = (s32[]{:T(128)}, f32[256,256]{1,0:T(8,128)S(1)}, s32[2,2]{1,0:T(2,128)S(1)}, f32[2,128,128]{2,1,0:T(8,128)S(1)}, s32[]{:T(128)}) while((s32[]{:T(128)}, f32[256,256]{1,0:T(8,128)S(1)}, s32[2,2]{1,0:T(2,128)S(1)}, f32[2,128,128]{2,1,0:T(8,128)S(1)}, s32[]{:T(128)}) %tuple.98), condition=%wide.while_cond, body=%wide.while_body.sunk | while | flops 2 | bytes 131189 | solution.py:52
  173.4 1.4 bitcast_dynamic-update-slice_fusion.2
  175.4 1.4 bitcast_dynamic-update-slice_fusion.2
  176.8 19.7 %custom-call.15 = f32[2,128,128]{1,2,0:T(8,128)S(1)} custom-call(f32[2,128,128]{2,1,0:T(8,128)S(1)} %get-tuple-element.165), custom_call_target="InvertDiagBlocksLowerTriangular" | custom-call | tf_op jit(solution)/shard_map/triangular_solve | solution.py:52
  197.1 0.6 fusion.47
  197.7 30.8 %all_gather.3 = bf16[512,256]{1,0:T(8,128)(2,1)S(1)} all-gather(bf16[64,256]{1,0:T(8,128)(2,1)S(1)} %get-tuple-element.217), channel_id=1, replica_groups=mesh['gx'=8,'yz'=4] {'gx'}, dimensions={0}, use_global_device_ids=true | all-gather | bytes 294912 | tf_op jit(solution)/shard_map/all_gather | solution.py:57
  228.5 0.7 reshape.128
  230.5 0.9 copy.26
  (72 shorter events, 5.6 us)
Async XLA Ops:
  7.2 53.5 %all-reduce.6.cloned.1.call-start = ((), (), s32[]{:S(2)}) async-start(), calls=%async_computation.1 | async-start | bytes 131072 | tf_op jit(solution)/shard_map/psum | solution.py:49
  7.2 0.7 copy-start.4
  11.0 0.8 copy-start.3
  26.1 0.6 copy-start.2
  30.1 198.4 %all-to-all-start = ((bf16[8,2,16384]{2,1,0:T(2,128)(2,1)}), bf16[8,2,16384]{2,1,0:T(2,128)(2,1)S(1)}, u32[]{:S(2)}, u32[]{:S(2)}) async-start(bf16[8,2,16384]{2,1,0:T(2,128)(2,1)} %reshape.127), calls=%async_computation | async-start | bytes 1048576 | tf_op jit(solution)/shard_map/all_to_all | solution.py:56
  37.4 98.1 %all-reduce.8.cloned.1.call-start = ((), (), s32[]{:S(2)}) async-start(), calls=%async_computation.2 | async-start | bytes 524288 | tf_op jit(solution)/shard_map/psum | solution.py:50
  62.7 0.8 copy-start.1
  135.5 1.2 copy-start
Sparse Core Ops, SparseCore 0:
  26.9 33.7 all-reduce.5
  64.9 70.5 all-reduce.7
where the time goes:
time: 239 us; the launch traced here: 238 us
  waiting for transfers between devices  95.1 us (40%)
  other arithmetic  60.9 us (25%)
  blocking collectives  30.8 us (13%)
  between operations  17.5 us (7%)
  local copies, waits for them, and re-layouts  13.9 us (6%)
  matrix products  9.83 us (4%)
  starting transfers between devices  7.51 us (3%)
  loops' own time  2.74 us (1%)
    psum x1, waiting for transfers between devices, local(): lax.psum(jnp.dot(sketch.T, sketch, precision=lax.Precision.HIGHEST), 'gx')  72 us
    another operation x6, other arithmetic, local(): cholesky_factor = jnp.linalg.cholesky(gram_matrix)  33.9 us
    all_gather x1, blocking collectives, local(): every_row = lax.all_gather(factor_bf, 'gx', axis=0, tiled=True)  30.8 us
    psum x1, waiting for transfers between devices, local(): sketch = lax.psum(partial_sketch, 'yz') * normalizer  23 us
    another operation x3, other arithmetic, local(): lax.linalg.triangular_solve(cholesky_factor, sketch, left_side=False, low...  19.7 us
    all_to_all x1, starting transfers between devices, local(): lax.all_to_all(tensor_slabs, 'gx', split_axis=2, concat_axis=0, tiled=True)  7.25 us
    unnamed x15, local copies, waits for them, and re-layouts  6.51 us
    dot_general x4, matrix products, add_slab(): jnp.dot(scaled, hadamard_part, preferred_element_type=jnp.float32)  6.37 us
  transfers between devices with their start and end apart: 3, of which 2 were waited for; matrix products, arithmetic and copies ran while one was open for 28% of the time, Pallas kernels for 0%

commit v1 on v0

v1 whole, which is shorter than its diff:
```python
import functools
import math

import jax
import jax.numpy as jnp
from jax import lax
from jax.experimental import pallas as pl
from jax.experimental.pallas import tpu as pltpu
from jax.sharding import PartitionSpec as P

MESH = pl.DeviceIdType.MESH
HIGHEST = lax.Precision.HIGHEST
F32 = jnp.float32
BF16 = jnp.bfloat16
LOW_BITS = 5
CORES = 2
PANEL = 64


def signs(index_count, picked):
    shared = jnp.bitwise_and(
        lax.broadcasted_iota(jnp.int32, (index_count, picked.shape[1]), 0), picked
    )
    for step in (16, 8, 4, 2, 1):
        shared = jnp.bitwise_xor(shared, jnp.right_shift(shared, step))
    return (1 - 2 * jnp.bitwise_and(shared, 1)).astype(F32)


def sketch_kernel(
    n_gx, n_yz, slab_total, moves,
    counts_ref, slabs_ref, scale_ref, samples_ref, *rest,
):
    sketch_ref = rest[0]
    if moves:
        moved_ref = rest[1]
        a2a_send, a2a_recv, own_sem = rest[-3:]
        rest = rest[:1] + rest[2:-3]
    (
        hada, part, arrived, rs_send, rs_recv, gx_send, gx_recv, y_send, y_recv, c_send, c_recv
    ) = rest[1:]
    gx, yz = lax.axis_index("gx"), lax.axis_index("yz")
    slots, rows, width = slabs_ref.shape
    n_y = n_yz // CORES
    core = yz % CORES
    y_pos = yz // CORES
    own_cols = width // n_gx
    chunk = rows // n_yz

    def gx_peer(step):
        return lax.rem(gx + step, n_gx)

    def yz_peer(step):
        return lax.rem(yz + step, n_yz)

    barrier = pltpu.get_barrier_semaphore()
    for step in range(1, n_gx):
        pl.semaphore_signal(barrier, inc=1, device_id=(gx_peer(step), yz), device_id_type=MESH)
    for step in range(1, n_yz):
        pl.semaphore_signal(barrier, inc=1, device_id=(gx, yz_peer(step)), device_id_type=MESH)
    pl.semaphore_wait(barrier, n_gx + n_yz - 2)

    def columns_of(index):
        return pl.ds(pl.multiple_of(index * own_cols, own_cols), own_cols)

    def rows_of(index):
        return pl.ds(pl.multiple_of(index * rows, rows), rows)

    a2a = []
    if moves:
        own_copy = pltpu.make_async_copy(
            slabs_ref.at[:, :, columns_of(gx)], moved_ref.at[:, rows_of(gx), :], own_sem
        )
        own_copy.start()
        for step in range(1, n_gx):
            peer = gx_peer(step)
            copy = pltpu.make_async_remote_copy(
                src_ref=slabs_ref.at[:, :, columns_of(peer)],
                dst_ref=moved_ref.at[:, rows_of(gx), :],
                send_sem=a2a_send.at[step - 1],
                recv_sem=a2a_recv.at[step - 1],
                device_id=(peer, yz),
                device_id_type=MESH,
            )
            copy.start()
            a2a.append(copy)

    offset = jnp.int32(0)
    own_count = jnp.int32(0)
    for group in range(counts_ref.shape[0]):
        count = counts_ref[group]
        offset = offset + jnp.where(group < yz, count, 0)
        own_count = own_count + jnp.where(group == yz, count, 0)

    low = 1 << LOW_BITS
    high = width // low
    total = None
    for slot in range(slots):
        slab = jnp.minimum(offset + slot, slab_total - 1)
        alive = (slot < own_count).astype(F32)
        picked = samples_ref[pl.ds(slab, 1), :]
        high_sign = signs(high, jnp.right_shift(picked, LOW_BITS))
        low_sign = signs(low, jnp.bitwise_and(picked, low - 1))
        for top in range(high):
            hada[top * low : (top + 1) * low, :] = (high_sign[top : top + 1, :] * low_sign).astype(BF16)
        scale = scale_ref[pl.ds(slab, 1), :] * alive
        scaled = (slabs_ref[slot].astype(F32) * scale).astype(BF16)
        term = jnp.dot(scaled, hada[...], preferred_element_type=F32)
        total = term if total is None else total + term
    part[...] = total * (1.0 / math.sqrt(slab_total * width))

    def chunk_of(index):
        return pl.ds(pl.multiple_of(index * chunk, chunk), chunk)

    reduce = []
    for step in range(1, n_yz):
        peer = yz_peer(step)
        copy = pltpu.make_async_remote_copy(
            src_ref=part.at[chunk_of(peer)],
            dst_ref=arrived.at[step - 1],
            send_sem=rs_send.at[step - 1],
            recv_sem=rs_recv.at[step - 1],
            device_id=(gx, peer),
            device_id_type=MESH,
        )
        copy.start()
        reduce.append(copy)
    own = part[chunk_of(yz)]
    for step in range(1, n_yz):
        reduce[step - 1].wait_recv()
        own = own + arrived[step - 1]

    def place(gx_index, yz_index):
        start = gx_index * rows + yz_index * chunk
        return sketch_ref.at[pl.ds(pl.multiple_of(start, chunk), chunk)]

    place(gx, yz)[...] = own
    sent = []
    over_gx = []
    for step in range(1, n_gx):
        copy = pltpu.make_async_remote_copy(
            src_ref=place(gx, yz),
            dst_ref=place(gx, yz),
            send_sem=gx_send.at[step - 1],
            recv_sem=gx_recv.at[step - 1],
            device_id=(gx_peer(step), yz),
            device_id_type=MESH,
        )
        copy.start()
        over_gx.append(copy)

    def to_y(gx_index, slot):
        for step in range(1, n_y):
            peer = lax.rem(y_pos + step, n_y) * CORES + core
            copy = pltpu.make_async_remote_copy(
                src_ref=place(gx_index, yz),
                dst_ref=place(gx_index, yz),
                send_sem=y_send.at[step - 1, slot],
                recv_sem=y_recv.at[step - 1, slot],
                device_id=(gx, peer),
                device_id_type=MESH,
            )
            copy.start()
            over_y.append(copy)

    def to_core(gx_index, yz_index, y_step, slot):
        copy = pltpu.make_async_remote_copy(
            src_ref=place(gx_index, yz_index),
            dst_ref=place(gx_index, yz_index),
            send_sem=c_send.at[y_step, slot],
            recv_sem=c_recv.at[y_step, slot],
            device_id=(gx, y_pos * CORES + 1 - core),
            device_id_type=MESH,
        )
        copy.start()
        over_core.append(copy)

    over_y = []
    over_core = []
    to_y(gx, 0)
    to_core(gx, yz, 0, 0)
    for step in range(1, n_gx):
        over_gx[step - 1].wait_recv()
        source = lax.rem(gx + n_gx - step, n_gx)
        to_y(source, step)
        to_core(source, yz, 0, step)
    for slot in range(n_gx):
        source = lax.rem(gx + n_gx - slot, n_gx)
        for step in range(1, n_y):
            over_y[slot * (n_y - 1) + step - 1].wait_recv()
            from_yz = lax.rem(y_pos + n_y - step, n_y) * CORES + core
            to_core(source, from_yz, step, slot)
    for copy in over_core:
        copy.wait()
    for copy in over_y + over_gx + reduce:
        copy.wait_send()
    for copy in a2a:
        copy.wait()
    if moves:
        own_copy.wait()


def factor_kernel(counts_ref, sketch_ref, moved_ref, basis_ref, core_ref, work):
    gx, yz = lax.axis_index("gx"), lax.axis_index("yz")
    rank = sketch_ref.shape[1]
    slots = moved_ref.shape[0]
    own_rows = basis_ref.shape[0]
    lanes, tile = 128, 8
    gram = lax.dot_general(
        sketch_ref[...], sketch_ref[...], (((0,), (0,)), ((), ())),
        precision=HIGHEST, preferred_element_type=F32,
    )
    work[:, :rank] = gram
    work[:, rank:] = (
        lax.broadcasted_iota(jnp.int32, (rank, rank), 0)
        == lax.broadcasted_iota(jnp.int32, (rank, rank), 1)
    ).astype(F32)
    sub = lax.broadcasted_iota(jnp.int32, (tile, lanes), 0)
    full = (tile, lanes)

    for start in range(0, rank, PANEL):
        end = min(start + PANEL, rank)
        for row in range(start, end, tile):
            at = row // lanes
            first = row % lanes
            used = list(range(at, rank // lanes)) + list(range(rank // lanes, rank // lanes + at + 1))
            block = work[row : row + tile, at * lanes : (at + 1) * lanes]
            g = [[None] * tile for _ in range(tile)]
            for j in range(tile):
                column = jnp.broadcast_to(block[:, first + j : first + j + 1], full)
                for i in range(j, tile):
                    g[i][j] = jnp.broadcast_to(column[i : i + 1, :], full)
            l = [[None] * tile for _ in range(tile)]
            v = [[None] * tile for _ in range(tile)]
            for j in range(tile):
                inverse = lax.rsqrt(g[j][j])
                v[j][j] = inverse
                for i in range(j + 1, tile):
                    l[i][j] = g[i][j] * inverse
                for i in range(j + 1, tile):
                    for k in range(j + 1, i + 1):
                        g[i][k] = g[i][k] - l[i][j] * l[k][j]
                for k in range(j):
                    inner = l[j][k] * v[k][k]
                    for m in range(k + 1, j):
                        inner = inner + l[j][m] * v[m][k]
                    v[j][k] = -inverse * inner
            v_columns = []
            for j in range(tile):
                column = jnp.zeros(full, F32)
                for i in range(j, tile):
                    column = jnp.where(sub == i, v[i][j], column)
                v_columns.append(column)
            spread = {}
            for n in used:
                there = work[row : row + tile, n * lanes : (n + 1) * lanes]
                done = v_columns[0] * jnp.broadcast_to(there[0:1, :], full)
                for j in range(1, tile):
                    done = done + v_columns[j] * jnp.broadcast_to(there[j : j + 1, :], full)
                work[row : row + tile, n * lanes : (n + 1) * lanes] = done
                spread[n] = [jnp.broadcast_to(done[j : j + 1, :], full) for j in range(tile)]
            for below in range(row + tile, end, tile):
                there = work[below : below + tile, at * lanes : (at + 1) * lanes]
                raw = [
                    jnp.broadcast_to(there[:, first + j : first + j + 1], full) for j in range(tile)
                ]
                left = []
                for j in range(tile):
                    value = raw[0] * v[j][0]
                    for k in range(1, j + 1):
                        value = value + raw[k] * v[j][k]
                    left.append(value)
                for n in used:
                    value = work[below : below + tile, n * lanes : (n + 1) * lanes]
                    for j in range(tile):
                        value = value - left[j] * spread[n][j]
                    work[below : below + tile, n * lanes : (n + 1) * lanes] = value
        if end < rank:
            from_lane = end // lanes * lanes
            left = work[start:end, from_lane:rank]
            right = work[start:end, from_lane:]
            update = lax.dot_general(
                left, right, (((0,), (0,)), ((), ())), precision=HIGHEST, preferred_element_type=F32
            )
            work[end:, from_lane:] = work[end:, from_lane:] - update[end - from_lane :, :]

    keep = (
        lax.broadcasted_iota(jnp.int32, (rank, rank), 0)
        >= lax.broadcasted_iota(jnp.int32, (rank, rank), 1)
    )
    inverse = jnp.where(keep, work[:, rank:], 0.0)
    basis_ref[...] = lax.dot_general(
        sketch_ref[pl.ds(pl.multiple_of(gx * own_rows, own_rows), own_rows), :], inverse,
        (((1,), (1,)), ((), ())), precision=HIGHEST, preferred_element_type=F32,
    )
    factor = lax.dot_general(
        inverse, sketch_ref[...], (((1,), (1,)), ((), ())),
        precision=HIGHEST, preferred_element_type=F32,
    ).astype(BF16)
    own_count = counts_ref[yz]
    for slot in range(slots):
        alive = (slot < own_count).astype(F32)
        projected = jnp.dot(factor, moved_ref[slot], preferred_element_type=F32)
        core_ref[slot] = (projected * alive).astype(BF16)


def local(n_gx, n_yz, tensor_slabs, slab_counts, column_scale, samples):
    rows, slots, width = tensor_slabs.shape
    rank = samples.shape[1]
    slab_total = column_scale.shape[0]
    n_y = n_yz // CORES
    chunk = rows // n_yz
    own_cols = width // n_gx
    vmem = pl.BlockSpec(memory_space=pltpu.VMEM)
    smem = pl.BlockSpec(memory_space=pltpu.SMEM)
    dma = pltpu.SemaphoreType.DMA
    moves = own_cols % 128 == 0
    found = pl.pallas_call(
        functools.partial(sketch_kernel, n_gx, n_yz, slab_total, moves),
        out_shape=(
            jax.ShapeDtypeStruct((rows * n_gx, rank), F32),
            jax.ShapeDtypeStruct((slots, rows * n_gx, own_cols), BF16),
        )[: 1 + moves],
        in_specs=[smem, vmem, vmem, vmem],
        out_specs=(vmem, vmem)[: 1 + moves],
        scratch_shapes=[
            pltpu.VMEM((width, rank), BF16),
            pltpu.VMEM((rows, rank), F32),
            pltpu.VMEM((n_yz - 1, chunk, rank), F32),
            dma((n_yz - 1,)), dma((n_yz - 1,)),
            dma((n_gx - 1,)), dma((n_gx - 1,)),
            dma((max(n_y - 1, 1), n_gx)), dma((max(n_y - 1, 1), n_gx)),
            dma((n_y, n_gx)), dma((n_y, n_gx)),
        ] + ([dma((n_gx - 1,)), dma((n_gx - 1,)), dma(())] if moves else []),
        compiler_params=pltpu.CompilerParams(
            collective_id=0, has_side_effects=True, vmem_limit_bytes=32 << 20
        ),
    )(slab_counts, jnp.transpose(tensor_slabs, (1, 0, 2)), column_scale, samples)
    sketch = found[0]
    if moves:
        moved = found[1]
    else:
        moved = jnp.transpose(
            lax.all_to_all(tensor_slabs, "gx", split_axis=2, concat_axis=0, tiled=True), (1, 0, 2)
        )
    basis_factor, core = pl.pallas_call(
        factor_kernel,
        out_shape=(
            jax.ShapeDtypeStruct((rows, rank), F32),
            jax.ShapeDtypeStruct((slots, rank, own_cols), BF16),
        ),
        in_specs=[smem, vmem, vmem],
        out_specs=(vmem, vmem),
        scratch_shapes=[pltpu.VMEM((rank, 2 * rank), F32)],
        compiler_params=pltpu.CompilerParams(vmem_limit_bytes=32 << 20),
    )(slab_counts, sketch, moved)
    return basis_factor, jnp.transpose(core, (1, 0, 2))


def solution(mesh):
    placed = (P("gx", "yz", None), P(), P(), P())
    return jax.shard_map(
        functools.partial(local, mesh.shape["gx"], mesh.shape["yz"]),
        mesh=mesh,
        in_specs=placed,
        out_specs=(P("gx", None), P(None, "yz", "gx")),
        check_vma=False,
    )
```

time: 239 us -> 43.4 us (0.18)
  waiting for transfers between devices: 95.1 us -> 0 us
  other arithmetic: 60.9 us -> 0 us
  Pallas kernels: 0 us -> 39.8 us
  blocking collectives: 30.8 us -> 0 us
  between operations: 17.5 us -> 0.69 us
  local copies, waits for them, and re-layouts: 13.9 us -> 2.76 us
  matrix products: 9.83 us -> 0 us
  starting transfers between devices: 7.51 us -> 0 us
  loops' own time: 2.74 us -> 0 us
    psum x2 -> x0, waiting for transfers between devices: 95 us -> none  [the longest x1 72 us: local(): lax.psum(jnp.dot(sketch.T, sketch, precision=lax.Precision.HIGHEST), 'gx')]
    another operation x9 -> x0, other arithmetic: 53.7 us -> none  [the longest x6 33.9 us: local(): cholesky_factor = jnp.linalg.cholesky(gram_matrix)]
    pallas_call x0 -> x2, Pallas kernels: none -> 39.8 us  [the longest x1 26.8 us: local(): pl.pallas_call(functools.partial(sketch_kernel, n_gx, n_yz, slab_total, m...]
    all_gather x1 -> x0, blocking collectives: 30.8 us -> none  [local(): every_row = lax.all_gather(factor_bf, 'gx', axis=0, tiled=True)]
    dot_general x6 -> x0, matrix products: 8.75 us -> none  [the longest x4 6.37 us: add_slab(): jnp.dot(scaled, hadamard_part, preferred_element_type=jnp.float32)]
    all_to_all x1 -> x0, starting transfers between devices: 7.25 us -> none  [local(): lax.all_to_all(tensor_slabs, 'gx', split_axis=2, concat_axis=0, tiled=True)]
    convert_element_type x6 -> x0, other arithmetic: 6.36 us -> none  [the longest x4 5.15 us: add_slab(): piece.astype(jnp.float32) * slab_scale[None, :]]
    another operation x9 -> x0, local copies, waits for them, and re-layouts: 4.05 us -> none
  transfers between devices with their start and end apart: 3 -> 0, of which waited for: 2 -> 0; matrix products, arithmetic and copies ran while one was open for 28% -> 0% of each run, Pallas kernels for 0% -> 0%
where the time goes in v1:
time: 43.4 us; the launch traced here: 43.2 us
  Pallas kernels  39.8 us (92%)
  local copies, waits for them, and re-layouts  2.76 us (6%)
  between operations  0.69 us (2%)
    pallas_call x1, Pallas kernels, local(): pl.pallas_call(functools.partial(sketch_kernel, n_gx, n_yz, slab_total, m...  26.8 us
    pallas_call x1, Pallas kernels, local(): pl.pallas_call(factor_kernel, out_shape=(jax.ShapeDtypeStruct((rows, rank...  13 us
    unnamed x8, local copies, waits for them, and re-layouts  2.76 us

profile of v1, /device:TPU:0, one launch (start us, length us, event | category | flops | bytes accessed | tf_op | source)
XLA Modules:
  0.0 43.2 jit_solution(5566448473337501770)
XLA Ops:
  0.6 0.0 copy-start.1
  0.6 0.0 copy-start
  0.6 1.2 %copy.9 = bf16[64,4,1024]{2,0,1:T(8,128)(2,1)S(1)} copy(bf16[64,4,1024]{2,1,0:T(4,128)(2,1)} %param.4) | data formatting | bytes 1048576 | tf_op args[0]
  1.9 0.0 copy-start.2
  1.9 0.0 copy-done.1
  1.9 0.0 copy-done
  1.9 0.6 %copy-done.2 = s32[4]{0:T(128)S(1)} copy-done((s32[4]{0:T(128)S(1)}, s32[4]{0:T(128)}, u32[]{:S(2)}) %copy-start.2) | copy-done | bytes 40
  2.5 26.8 %shard_map.59 = (f32[512,256]{1,0:T(8,128)S(1)}, bf16[4,512,128]{2,1,0:T(8,128)(2,1)S(1)}) custom-call(s32[4]{0:T(128)S(1)} %copy-done.2, bf16[4,64,1024]{2,1,0:T(8,128)(2,1)S(1)} %bitcast.4, f32[8,1024]{1,0:T(8,128)S(1)} %copy-done, s32[8,256]{1,0:T(8,128)S(1)} %copy-done.1), custom_call_target="tpu_custom_call" | custom-call | tf_op jit(solution)/shard_map/pallas_call | solution.py:317
  29.4 13.0 %shard_map.60 = (f32[64,256]{1,0:T(8,128)}, bf16[4,256,128]{2,1,0:T(8,128)(2,1)S(1)}) custom-call(s32[4]{0:T(128)S(1)} %copy-done.2, f32[512,256]{1,0:T(8,128)S(1)} %get-tuple-element.6.sketch_ref, bf16[4,512,128]{2,1,0:T(8,128)(2,1)S(1)} %get-tuple-element.7.moved_ref), custom_call_target="tpu_custom_call" | custom-call | tf_op jit(solution)/shard_map/pallas_call | solution.py:345
  42.3 0.9 %copy.7 = bf16[256,4,128]{2,1,0:T(4,128)(2,1)} copy(bf16[256,4,128]{2,0,1:T(8,128)(2,1)S(1)} %bitcast.5) | data formatting | bytes 524288
Async XLA Ops:
  0.6 1.2 %copy-start.1 = (s32[8,256]{1,0:T(8,128)S(1)}, s32[8,256]{1,0:T(8,128)}, u32[]{:S(2)}) copy-start(s32[8,256]{1,0:T(8,128)} %samples_ref.1) | copy-start | bytes 24580
  0.6 1.2 %copy-start = (f32[8,1024]{1,0:T(8,128)S(1)}, f32[8,1024]{1,0:T(8,128)}, u32[]{:S(2)}) copy-start(f32[8,1024]{1,0:T(8,128)} %scale_ref.1) | copy-start | bytes 98308
  1.9 0.7 %copy-start.2 = (s32[4]{0:T(128)S(1)}, s32[4]{0:T(128)}, u32[]{:S(2)}) copy-start(s32[4]{0:T(128)} %counts_ref.3) | copy-start | bytes 52

commit v2 on v1

--- a/solution.py
+++ b/solution.py
@@ -30,14 +30,16 @@
     n_gx, n_yz, slab_total, moves,
     counts_ref, slabs_ref, scale_ref, samples_ref, *rest,
 ):
-    sketch_ref = rest[0]
     if moves:
-        moved_ref = rest[1]
-        a2a_send, a2a_recv, own_sem = rest[-3:]
-        rest = rest[:1] + rest[2:-3]
+        moved_ref, a2a_send, a2a_recv, own_sem = rest[-4:]
+        rest = rest[:-4]
+    else:
+        moved_ref = rest[0]
+        rest = rest[1:]
     (
-        hada, part, arrived, rs_send, rs_recv, gx_send, gx_recv, y_send, y_recv, c_send, c_recv
-    ) = rest[1:]
+        basis_ref, core_ref, sketch_ref, work, hada, part, arrived,
+        rs_send, rs_recv, gx_send, gx_recv, y_send, y_recv, c_send, c_recv,
+    ) = rest
     gx, yz = lax.axis_index("gx"), lax.axis_index("yz")
     slots, rows, width = slabs_ref.shape
     n_y = n_yz // CORES
@@ -64,25 +66,6 @@
 
     def rows_of(index):
         return pl.ds(pl.multiple_of(index * rows, rows), rows)
-
-    a2a = []
-    if moves:
-        own_copy = pltpu.make_async_copy(
-            slabs_ref.at[:, :, columns_of(gx)], moved_ref.at[:, rows_of(gx), :], own_sem
-        )
-        own_copy.start()
-        for step in range(1, n_gx):
-            peer = gx_peer(step)
-            copy = pltpu.make_async_remote_copy(
-                src_ref=slabs_ref.at[:, :, columns_of(peer)],
-                dst_ref=moved_ref.at[:, rows_of(gx), :],
-                send_sem=a2a_send.at[step - 1],
-                recv_sem=a2a_recv.at[step - 1],
-                device_id=(peer, yz),
-                device_id_type=MESH,
-            )
-            copy.start()
-            a2a.append(copy)
 
     offset = jnp.int32(0)
     own_count = jnp.int32(0)
@@ -134,7 +117,6 @@
         return sketch_ref.at[pl.ds(pl.multiple_of(start, chunk), chunk)]
 
     place(gx, yz)[...] = own
-    sent = []
     over_gx = []
     for step in range(1, n_gx):
         copy = pltpu.make_async_remote_copy(
@@ -189,20 +171,42 @@
             over_y[slot * (n_y - 1) + step - 1].wait_recv()
             from_yz = lax.rem(y_pos + n_y - step, n_y) * CORES + core
             to_core(source, from_yz, step, slot)
+    a2a = []
+    if moves:
+        own_copy = pltpu.make_async_copy(
+            slabs_ref.at[:, :, columns_of(gx)], moved_ref.at[:, rows_of(gx), :], own_sem
+        )
+        own_copy.start()
+        for step in range(1, n_gx):
+            peer = gx_peer(step)
+            copy = pltpu.make_async_remote_copy(
+                src_ref=slabs_ref.at[:, :, columns_of(peer)],
+                dst_ref=moved_ref.at[:, rows_of(gx), :],
+                send_sem=a2a_send.at[step - 1],
+                recv_sem=a2a_recv.at[step - 1],
+                device_id=(peer, yz),
+                device_id_type=MESH,
+            )
+            copy.start()
+            a2a.append(copy)
     for copy in over_core:
         copy.wait()
     for copy in over_y + over_gx + reduce:
         copy.wait_send()
+    factor = factorise(sketch_ref, basis_ref, work)
     for copy in a2a:
         copy.wait()
     if moves:
         own_copy.wait()
-
-
-def factor_kernel(counts_ref, sketch_ref, moved_ref, basis_ref, core_ref, work):
-    gx, yz = lax.axis_index("gx"), lax.axis_index("yz")
+    for slot in range(slots):
+        alive = (slot < own_count).astype(F32)
+        projected = jnp.dot(factor, moved_ref[slot], preferred_element_type=F32)
+        core_ref[slot] = (projected * alive).astype(BF16)
+
+
+def factorise(sketch_ref, basis_ref, work):
+    gx = lax.axis_index("gx")
     rank = sketch_ref.shape[1]
-    slots = moved_ref.shape[0]
     own_rows = basis_ref.shape[0]
     lanes, tile = 128, 8
     gram = lax.dot_general(
@@ -292,15 +296,10 @@
         sketch_ref[pl.ds(pl.multiple_of(gx * own_rows, own_rows), own_rows), :], inverse,
         (((1,), (1,)), ((), ())), precision=HIGHEST, preferred_element_type=F32,
     )
-    factor = lax.dot_general(
+    return lax.dot_general(
         inverse, sketch_ref[...], (((1,), (1,)), ((), ())),
         precision=HIGHEST, preferred_element_type=F32,
     ).astype(BF16)
-    own_count = counts_ref[yz]
-    for slot in range(slots):
-        alive = (slot < own_count).astype(F32)
-        projected = jnp.dot(factor, moved_ref[slot], preferred_element_type=F32)
-        core_ref[slot] = (projected * alive).astype(BF16)
 
 
 def local(n_gx, n_yz, tensor_slabs, slab_counts, column_scale, samples):
@@ -314,15 +313,30 @@
     smem = pl.BlockSpec(memory_space=pltpu.SMEM)
     dma = pltpu.SemaphoreType.DMA
     moves = own_cols % 128 == 0
-    found = pl.pallas_call(
+    every = rows * n_gx
+    operands = [slab_counts, jnp.transpose(tensor_slabs, (1, 0, 2)), column_scale, samples]
+    exchange = [
+        pltpu.VMEM((slots, every, own_cols), BF16), dma((n_gx - 1,)), dma((n_gx - 1,)), dma(())
+    ]
+    if not moves:
+        operands.append(
+            jnp.transpose(
+                lax.all_to_all(tensor_slabs, "gx", split_axis=2, concat_axis=0, tiled=True),
+                (1, 0, 2),
+            )
+        )
+        exchange = []
+    basis_factor, core = pl.pallas_call(
         functools.partial(sketch_kernel, n_gx, n_yz, slab_total, moves),
         out_shape=(
-            jax.ShapeDtypeStruct((rows * n_gx, rank), F32),
-            jax.ShapeDtypeStruct((slots, rows * n_gx, own_cols), BF16),
-        )[: 1 + moves],
-        in_specs=[smem, vmem, vmem, vmem],
-        out_specs=(vmem, vmem)[: 1 + moves],
+            jax.ShapeDtypeStruct((rows, rank), F32),
+            jax.ShapeDtypeStruct((slots, rank, own_cols), BF16),
+        ),
+        in_specs=[smem] + [vmem] * (len(operands) - 1),
+        out_specs=(vmem, vmem),
         scratch_shapes=[
+            pltpu.VMEM((every, rank), F32),
+            pltpu.VMEM((rank, 2 * rank), F32),
             pltpu.VMEM((width, rank), BF16),
             pltpu.VMEM((rows, rank), F32),
             pltpu.VMEM((n_yz - 1, chunk, rank), F32),
@@ -330,29 +344,11 @@
             dma((n_gx - 1,)), dma((n_gx - 1,)),
             dma((max(n_y - 1, 1), n_gx)), dma((max(n_y - 1, 1), n_gx)),
             dma((n_y, n_gx)), dma((n_y, n_gx)),
-        ] + ([dma((n_gx - 1,)), dma((n_gx - 1,)), dma(())] if moves else []),
+        ] + exchange,
         compiler_params=pltpu.CompilerParams(
             collective_id=0, has_side_effects=True, vmem_limit_bytes=32 << 20
         ),
-    )(slab_counts, jnp.transpose(tensor_slabs, (1, 0, 2)), column_scale, samples)
-    sketch = found[0]
-    if moves:
-        moved = found[1]
-    else:
-        moved = jnp.transpose(
-            lax.all_to_all(tensor_slabs, "gx", split_axis=2, concat_axis=0, tiled=True), (1, 0, 2)
-        )
-    basis_factor, core = pl.pallas_call(
-        factor_kernel,
-        out_shape=(
-            jax.ShapeDtypeStruct((rows, rank), F32),
-            jax.ShapeDtypeStruct((slots, rank, own_cols), BF16),
-        ),
-        in_specs=[smem, vmem, vmem],
-        out_specs=(vmem, vmem),
-        scratch_shapes=[pltpu.VMEM((rank, 2 * rank), F32)],
-        compiler_params=pltpu.CompilerParams(vmem_limit_bytes=32 << 20),
-    )(slab_counts, sketch, moved)
+    )(*operands)
     return basis_factor, jnp.transpose(core, (1, 0, 2))
 
 

time: 43.4 us -> 35.7 us (0.82)
  Pallas kernels: 39.8 us -> 31.4 us
  local copies, waits for them, and re-layouts: 2.76 us -> 3.39 us
    pallas_call x1 -> x0, Pallas kernels: 13 us -> none  [local(): pl.pallas_call(factor_kernel, out_shape=(jax.ShapeDtypeStruct((rows, rank...]
    pallas_call x1, Pallas kernels: 26.8 us -> 31.4 us  [local(): pl.pallas_call(functools.partial(sketch_kernel, n_gx, n_yz, slab_total, m...]
    unnamed x8 -> x9, local copies, waits for them, and re-layouts: 2.76 us -> 3.39 us
where the time goes in v2:
time: 35.7 us; the launch traced here: 35.5 us
  Pallas kernels  31.4 us (88%)
  local copies, waits for them, and re-layouts  3.39 us (9%)
  between operations  0.68 us (2%)
    pallas_call x1, Pallas kernels, local(): pl.pallas_call(functools.partial(sketch_kernel, n_gx, n_yz, slab_total, m...  31.4 us
    unnamed x9, local copies, waits for them, and re-layouts  3.39 us

profile of v2, /device:TPU:0, one launch (start us, length us, event | category | flops | bytes accessed | tf_op | source)
XLA Modules:
  0.0 35.5 jit_solution(10763241383774813649)
XLA Ops:
  0.6 0.0 copy-start.1
  0.6 0.0 copy-start
  0.6 1.2 %copy.9 = bf16[64,4,1024]{2,0,1:T(8,128)(2,1)S(1)} copy(bf16[64,4,1024]{2,1,0:T(4,128)(2,1)} %param.4) | data formatting | bytes 1048576 | tf_op args[0]
  1.9 0.0 copy-start.2
  1.9 0.0 copy-done.1
  1.9 0.0 copy-done
  1.9 0.6 %copy-done.2 = s32[4]{0:T(128)S(1)} copy-done((s32[4]{0:T(128)S(1)}, s32[4]{0:T(128)}, u32[]{:S(2)}) %copy-start.2) | copy-done | bytes 40
  2.5 31.4 %shard_map.59 = (f32[64,256]{1,0:T(8,128)S(1)}, bf16[4,256,128]{2,1,0:T(8,128)(2,1)S(1)}) custom-call(s32[4]{0:T(128)S(1)} %copy-done.2, bf16[4,64,1024]{2,1,0:T(8,128)(2,1)S(1)} %bitcast.4, f32[8,1024]{1,0:T(8,128)S(1)} %copy-done, s32[8,256]{1,0:T(8,128)S(1)} %copy-done.1), custom_call_target="tpu_custom_call" | custom-call | tf_op jit(solution)/shard_map/pallas_call | solution.py:329
  34.0 0.9 %copy.7 = bf16[256,4,128]{2,1,0:T(4,128)(2,1)} copy(bf16[256,4,128]{2,0,1:T(8,128)(2,1)S(1)} %bitcast.5) | data formatting | bytes 524288
  34.9 0.6 %copy.11 = f32[64,256]{1,0:T(8,128)} copy(f32[64,256]{1,0:T(8,128)S(1)} %get-tuple-element.10) | data formatting | bytes 131072
Async XLA Ops:
  0.6 1.2 %copy-start.1 = (s32[8,256]{1,0:T(8,128)S(1)}, s32[8,256]{1,0:T(8,128)}, u32[]{:S(2)}) copy-start(s32[8,256]{1,0:T(8,128)} %samples_ref.1) | copy-start | bytes 24580
  0.6 1.2 %copy-start = (f32[8,1024]{1,0:T(8,128)S(1)}, f32[8,1024]{1,0:T(8,128)}, u32[]{:S(2)}) copy-start(f32[8,1024]{1,0:T(8,128)} %scale_ref.1) | copy-start | bytes 98308
  1.9 0.7 %copy-start.2 = (s32[4]{0:T(128)S(1)}, s32[4]{0:T(128)}, u32[]{:S(2)}) copy-start(s32[4]{0:T(128)} %counts_ref.1) | copy-start | bytes 52
